TPU v7x, 32 devices: a whole 2x2x4 slice. The times are simulated.
32 devices in a mesh: groups: 2 (over x), aux: 16 (over z, y, core).
Axes of the slice: x: 2, y: 2, z: 4, core: 2. Of those that a mesh axis runs over, the one named last changes fastest.
Arguments:
- b_factors: bfloat16 [32, 850, 4096], P('groups', None, 'aux'), parts along dimension 0, may hold values from -0.75 to 0.75
- occ_energy: float32 [32], P('groups'), parts along dimension 0, may hold values from -1.2 to -0.4
- vir_energy: float32 [1700], P('groups'), parts along dimension 0, may hold values from 0.2 to 2.5
- kept: int32 [32], P('groups'), parts along dimension 0, may hold values 0 or 1
Outputs:
- gamma: bfloat16 [32, 850, 4096], P('groups', None, 'aux'), parts along dimension 0
There are 2 independent parts, one for each index of `groups`. A program takes and returns all parts, laid end to end along the dimension named above; each array names one. Nothing has to cross between parts.
Inputs may be any that keep to these rules, and one draw needn't show every extreme that they name: kept[i] = 1 keeps the pair of orbitals i and i + 1 modulo 16.
All inputs are finite; a program needn't handle non-finite values.
Results may differ from a plain program's by a relative error of at most 0.0045.
Values may be sent and summed in bfloat16 or wider, within the bound.
A program may use at most 192 MiB of HBM per device.

v0:
```python
import jax
import jax.numpy as jnp
from jax import lax
from jax.sharding import PartitionSpec as P


def passed_along(block, axis, distance):
    devices = range(lax.axis_size(axis))
    route = [((i - distance) % len(devices), i) for i in devices]
    return lax.ppermute(block, axis, route)


def amplitudes(left, right, e_left, e_right, vir_energy):
    coulomb = lax.dot_general(
        left, right, (((1,), (1,)), ((), ())), preferred_element_type=jnp.float32
    )
    denom = e_left + e_right - vir_energy[:, None] - vir_energy[None, :]
    t_pair = coulomb / denom
    return (2.0 * t_pair - t_pair.T).astype(jnp.bfloat16)


def body(b_factors, occ_energy, vir_energy, kept):
    owned = lax.all_to_all(b_factors, "aux", split_axis=0, concat_axis=2, tiled=True)[0]
    index = lax.axis_index("aux")
    count = lax.axis_size("aux")
    later = (index + 1) % count
    e_own = lax.dynamic_index_in_dim(occ_energy, index, 0, False)
    e_after = lax.dynamic_index_in_dim(occ_energy, later, 0, False)
    flag = lax.dynamic_index_in_dim(kept, index, 0, False)
    after = passed_along(owned, "aux", -1)
    u_own = amplitudes(owned, owned, e_own, e_own, vir_energy)
    diag = jnp.dot(u_own, owned, preferred_element_type=jnp.float32)
    zeros = jnp.zeros(owned.shape, jnp.float32)

    def with_pair(unused):
        u_pair = amplitudes(owned, after, e_own, e_after, vir_energy)
        mine = jnp.dot(u_pair, after, preferred_element_type=jnp.float32)
        theirs = lax.dot_general(
            u_pair, owned, (((0,), (0,)), ((), ())), preferred_element_type=jnp.float32
        )
        return (mine, theirs)

    def without(unused):
        return (zeros, zeros)

    mine, theirs = lax.cond(flag == 1, with_pair, without, 0)
    incoming = passed_along(theirs.astype(jnp.bfloat16), "aux", 1).astype(theirs.dtype)
    gamma = (diag + mine + incoming).astype(jnp.bfloat16)
    return lax.all_to_all(gamma[None], "aux", split_axis=2, concat_axis=0, tiled=True)


def solution(mesh):
    placed = (P("groups", None, "aux"), P("groups"), P("groups"), P("groups"))
    return jax.shard_map(
        body, mesh=mesh, in_specs=placed, out_specs=P("groups", None, "aux"), check_vma=False
    )
```

profile of v0, /device:TPU:1, one launch (start us, length us, event | category | flops | bytes accessed | tf_op | source)
XLA Modules:
  0.0 813.8 jit_solution(11004501821801861470)
XLA Ops:
  0.0 5.4 copy.19
  5.4 161.4 %all_to_all.33 = bf16[16,850,256]{2,1,0:T(8,128)(2,1)S(1)} all-to-all(bf16[16,850,256]{2,1,0:T(8,128)(2,1)S(1)} %copy.19), channel_id=1, replica_groups=mesh['groups'=2,'aux'=16] {'aux'}, dimensions={0} | all-to-all | bytes 13926400 | tf_op jit(solution)/shard_map/all_to_all | solution.py:23
  166.8 0.0 copy-start
  166.8 1.4 copy.29
  168.3 1.4 copy-done
  169.6 0.5 pad
  170.1 0.0 copy-start.4
  170.1 0.0 copy-start.3
  170.1 0.0 copy-start.2
  170.1 7.5 copy.27
  177.7 0.0 collective-permute-start
  177.7 0.0 copy-done.4
  177.7 0.6 dynamic_slice.15
  178.3 0.0 copy-done.3
  178.3 0.6 dynamic_slice.16
  179.6 76.6 %collective-permute-done = bf16[850,4096]{1,0:T(8,128)(2,1)} collective-permute-done((bf16[850,4096]{1,0:T(8,128)(2,1)}, bf16[850,4096]{1,0:T(8,128)(2,1)}, u32[]{:S(2)}, u32[]{:S(2)}) %collective-permute-start) | collective-permute-done | bytes 6963232 | tf_op jit(solution)/shard_map/ppermute | solution.py:10
  256.1 0.0 copy-done.2
  256.1 13.7 %conditional.1 = (f32[850,4096]{1,0:T(8,128)}, f32[850,4096]{1,0:T(8,128)}) conditional(s32[]{:T(128)} %bitcast.9, () %tuple.22, (bf16[850,4096]{1,0:T(8,128)(2,1)}, bf16[850,4096]{1,0:T(8,128)(2,1)}, s32[]{:T(128)}, f32[16]{0:T(128)S(1)}, f32[]{:T(128)}, /*index=5*/f32[850]{0:T(1024)S(1)}, s32[]{:T(128)}) %tuple.30), branch_computations={%region_0.1_spmd, %region_1.2_spmd.clone} | conditional | flops 17766277120 | bytes 87516224 | solution.py:46
  256.1 6.8 broadcast_in_dim.2
  262.9 6.8 broadcast_in_dim.2.clone
  269.9 9.0 %convert_element_type.27 = bf16[850,4096]{1,0:T(8,128)(2,1)} convert(f32[850,4096]{1,0:T(8,128)} %get-tuple-element.125) | non-fusion elementwise | flops 3481600 | bytes 20889600 | tf_op jit(solution)/shard_map/convert_element_type | solution.py:47
  278.9 31.9 %collective-permute-start.1 = (bf16[850,4096]{1,0:T(8,128)(2,1)}, bf16[850,4096]{1,0:T(8,128)(2,1)}, u32[]{:S(2)}, u32[]{:S(2)}) collective-permute-start(bf16[850,4096]{1,0:T(8,128)(2,1)} %convert_element_type.27), channel_id=1, source_target_pairs={{15,0},{0,1},{1,2},{2,3},{3,4},{4,5},{5,6},{6,7},{7,8},{8,9},{9,10... | collective-permute-start | bytes 20889608 | tf_op jit(solution)/shard_map/ppermute | solution.py:10
  312.0 10.8 %fusion.7 = f32[850,850,1]{1,0,2:T(8,128)S(1)} fusion(bf16[16,850,256]{2,1,0:T(8,128)(2,1)} %copy-done), kind=kOutput, calls=%fused_computation.8 | convolution fusion | flops 5918720000 | bytes 9853200 | tf_op jit(solution)/shard_map/dot_general | solution.py:14
  322.8 3.0 copy.20
  325.8 12.2 %fusion.11 = f32[850,4096]{1,0:T(8,128)S(1)} fusion(bf16[850,4096]{1,0:T(8,128)(2,1)} %bitcast.22, f32[850,850,1]{1,0,2:T(8,128)S(1)} %fusion.7, f32[850,850]{0,1:T(8,128)} %copy.20, f32[850]{0:T(1024)S(1)} %copy-done.2, f32[850]{0:T(1024)S(1)} %broadcast_subtract_fusion.1), kind=kOutput, calls=%fused_computation.14 | convolution fusion | flops 5923777536 | bytes 26676400 | tf_op jit(solution)/shard_map/dot_general | solution.py:32
  337.9 48.8 %collective-permute-done.1 = bf16[850,4096]{1,0:T(8,128)(2,1)} collective-permute-done((bf16[850,4096]{1,0:T(8,128)(2,1)}, bf16[850,4096]{1,0:T(8,128)(2,1)}, u32[]{:S(2)}, u32[]{:S(2)}) %collective-permute-start.1) | collective-permute-done | bytes 6963232 | tf_op jit(solution)/shard_map/ppermute | solution.py:10
  386.7 11.4 %fusion.6 = bf16[1,850,4096]{2,1,0:T(8,128)(2,1)} fusion(bf16[850,4096]{1,0:T(8,128)(2,1)} %collective-permute-done.1, f32[850,4096]{1,0:T(8,128)S(1)} %fusion.11, f32[850,4096]{1,0:T(8,128)} %get-tuple-element.124), kind=kLoop, calls=%fused_computation.7 | loop fusion | flops 13926400 | bytes 41779200 | tf_op jit(solution)/shard_map/broadcast_in_dim | solution.py:49
  398.1 32.1 %copy.22 = bf16[1,850,4096]{1,0,2:T(2,128)(2,1)} copy(bf16[1,850,4096]{2,1,0:T(8,128)(2,1)} %fusion.6) | data formatting | bytes 13926400 | tf_op jit(solution)/shard_map/broadcast_in_dim | solution.py:49
  430.2 0.5 broadcast.38
  430.7 157.7 %reduce = bf16[4096,850]{1,0:T(8,128)(2,1)} reduce(bf16[4096,1,850]{2,1,0:T(2,128)(2,1)} %bitcast.48, bf16[]{:T(256)} %broadcast.38), dimensions={1}, to_apply=%bitcast.40.reduce_sub_computation | reduce | bytes 13926402
  588.3 23.1 %reshape.19 = bf16[16,2,108800]{2,1,0:T(2,128)(2,1)} reshape(bf16[4096,850]{1,0:T(8,128)(2,1)} %reduce) | data formatting | bytes 13926400
  611.4 159.2 %all_to_all.34 = bf16[16,2,108800]{2,1,0:T(2,128)(2,1)} all-to-all(bf16[16,2,108800]{2,1,0:T(2,128)(2,1)} %reshape.19), channel_id=1, replica_groups=mesh['groups'=2,'aux'=16] {'aux'}, dimensions={0} | all-to-all | bytes 13926400 | tf_op jit(solution)/shard_map/all_to_all | solution.py:49
  770.6 21.3 %reshape.20 = bf16[4096,1,850]{2,1,0:T(2,128)(2,1)} reshape(bf16[16,2,108800]{2,1,0:T(2,128)(2,1)} %all_to_all.34) | data formatting | bytes 13926400
  792.0 9.3 %copy.26 = bf16[1,850,4096]{1,2,0:T(8,128)(2,1)} copy(bf16[1,850,4096]{1,0,2:T(2,128)(2,1)} %bitcast.49) | data formatting | bytes 13926400
  801.3 12.0 %copy.24 = bf16[1,850,16,256]{3,2,1,0:T(8,128)(2,1)} copy(bf16[1,850,16,256]{1,3,2,0:T(8,128)(2,1)} %bitcast.50) | data formatting | bytes 13926400 | tf_op jit(solution)/shard_map/all_to_all | solution.py:49
  (1 shorter events, 0.0 us)
Async XLA Ops:
  166.8 2.8 copy-start
  170.1 7.6 copy-start.4
  170.1 8.2 %copy-start.3 = (s32[16]{0:T(128)S(1)}, s32[16]{0:T(128)}, u32[]{:S(2)}) copy-start(s32[16]{0:T(128)} %param.9) | copy-start | bytes 196
  170.1 86.0 %copy-start.2 = (f32[850]{0:T(1024)S(1)}, f32[850]{0:T(1024)}, u32[]{:S(2)}) copy-start(f32[850]{0:T(1024)} %param.8) | copy-start | bytes 10204
  177.7 78.4 %collective-permute-start = (bf16[850,4096]{1,0:T(8,128)(2,1)}, bf16[850,4096]{1,0:T(8,128)(2,1)}, u32[]{:S(2)}, u32[]{:S(2)}) collective-permute-start(bf16[850,4096]{1,0:T(8,128)(2,1)} %bitcast.22), channel_id=1, source_target_pairs={{1,0},{2,1},{3,2},{4,3},{5,4},{6,5},{7,6},{8,7},{9,8},{10,9},{11,1... | collective-permute-start | bytes 20889608 | tf_op jit(solution)/shard_map/ppermute | solution.py:10
  278.9 107.9 %collective-permute-start.1 = (bf16[850,4096]{1,0:T(8,128)(2,1)}, bf16[850,4096]{1,0:T(8,128)(2,1)}, u32[]{:S(2)}, u32[]{:S(2)}) collective-permute-start(bf16[850,4096]{1,0:T(8,128)(2,1)} %convert_element_type.27), channel_id=1, source_target_pairs={{15,0},{0,1},{1,2},{2,3},{3,4},{4,5},{5,6},{6,7},{7,8},{8,9},{9,10... | collective-permute-start | bytes 20889608 | tf_op jit(solution)/shard_map/ppermute | solution.py:10
where the time goes:
time: 828 us; the launch traced here: 814 us
  blocking collectives  321 us (39%)
  other arithmetic  178 us (21%)
  local copies, waits for them, and re-layouts  132 us (16%)
  waiting for transfers between devices  125 us (15%)
  starting transfers between devices  31.9 us (4%)
  matrix products  22.9 us (3%)
    all_to_all x1, blocking collectives, body(): lax.all_to_all(b_factors, 'aux', split_axis=0, concat_axis=2, tiled=True)[0]  161 us
    all_to_all x1, blocking collectives, body(): lax.all_to_all(gamma[None], 'aux', split_axis=2, concat_axis=0, tiled=True)  159 us
    unnamed x1, other arithmetic  158 us
    ppermute x2, waiting for transfers between devices, passed_along(): return lax.ppermute(block, axis, route)  125 us
    unnamed x15, local copies, waits for them, and re-layouts  69.1 us
    broadcast_in_dim x1, local copies, waits for them, and re-layouts, body(): gamma[None]  32.1 us
    ppermute x2, starting transfers between devices, passed_along(): return lax.ppermute(block, axis, route)  31.9 us
  transfers between devices with their start and end apart: 2, of which 2 were waited for; matrix products, arithmetic and copies ran while one was open for 3% of the time, Pallas kernels for 0%

commit v1 on v0

--- a/solution.py
+++ b/solution.py
@@ -30,7 +30,7 @@
     after = passed_along(owned, "aux", -1)
     u_own = amplitudes(owned, owned, e_own, e_own, vir_energy)
     diag = jnp.dot(u_own, owned, preferred_element_type=jnp.float32)
-    zeros = jnp.zeros(owned.shape, jnp.float32)
+    zeros = jnp.zeros(owned.shape, jnp.bfloat16)
 
     def with_pair(unused):
         u_pair = amplitudes(owned, after, e_own, e_after, vir_energy)
@@ -38,15 +38,17 @@
         theirs = lax.dot_general(
             u_pair, owned, (((0,), (0,)), ((), ())), preferred_element_type=jnp.float32
         )
-        return (mine, theirs)
+        return (mine.astype(jnp.bfloat16), theirs.astype(jnp.bfloat16))
 
     def without(unused):
         return (zeros, zeros)
 
     mine, theirs = lax.cond(flag == 1, with_pair, without, 0)
-    incoming = passed_along(theirs.astype(jnp.bfloat16), "aux", 1).astype(theirs.dtype)
+    mine = mine.astype(jnp.float32)
+    incoming = passed_along(theirs, "aux", 1).astype(jnp.float32)
     gamma = (diag + mine + incoming).astype(jnp.bfloat16)
-    return lax.all_to_all(gamma[None], "aux", split_axis=2, concat_axis=0, tiled=True)
+    sliced = gamma.reshape(gamma.shape[0], count, -1).transpose(1, 0, 2)
+    return lax.all_to_all(sliced, "aux", split_axis=0, concat_axis=0, tiled=True)
 
 
 def solution(mesh):

time: 828 us -> 576 us (0.70)
  other arithmetic: 178 us -> 12.7 us
  local copies, waits for them, and re-layouts: 132 us -> 46.9 us
    unnamed x1 -> x0, other arithmetic: 158 us -> none
    unnamed x15 -> x12, local copies, waits for them, and re-layouts: 69.1 us -> 17.5 us
    broadcast_in_dim x3 -> x2, local copies, waits for them, and re-layouts: 45.7 us -> 10.6 us  [body(): zeros = jnp.zeros(owned.shape, jnp.bfloat16)]
    broadcast_in_dim x1 -> x0, other arithmetic: 11.4 us -> none  [body(): gamma[None]]
    reshape x0 -> x2, local copies, waits for them, and re-layouts: none -> 8.82 us  [body(): sliced = gamma.reshape(gamma.shape[0], count, -1).transpose(1, 0, 2)]
  transfers between devices with their start and end apart: 2 -> 2, of which waited for: 2 -> 2; matrix products, arithmetic and copies ran while one was open for 3% -> 5% of each run, Pallas kernels for 0% -> 0%
where the time goes in v1:
time: 576 us; the launch traced here: 566 us
  blocking collectives  321 us (56%)
  waiting for transfers between devices  122 us (21%)
  local copies, waits for them, and re-layouts  46.9 us (8%)
  starting transfers between devices  34 us (6%)
  matrix products  25.9 us (4%)
  other arithmetic  12.7 us (2%)
    all_to_all x1, blocking collectives, body(): lax.all_to_all(b_factors, 'aux', split_axis=0, concat_axis=2, tiled=True)[0]  161 us
    all_to_all x1, blocking collectives, body(): lax.all_to_all(sliced, 'aux', split_axis=0, concat_axis=0, tiled=True)  160 us
    ppermute x2, waiting for transfers between devices, passed_along(): return lax.ppermute(block, axis, route)  122 us
    ppermute x2, starting transfers between devices, passed_along(): return lax.ppermute(block, axis, route)  34 us
    unnamed x12, local copies, waits for them, and re-layouts  17.5 us
    dot_general x1, matrix products, body(): diag = jnp.dot(u_own, owned, preferred_element_type=jnp.float32)  15.1 us
    convert_element_type x1, other arithmetic, body(): gamma = (diag + mine + incoming).astype(jnp.bfloat16)  12.7 us
  transfers between devices with their start and end apart: 2, of which 2 were waited for; matrix products, arithmetic and copies ran while one was open for 5% of the time, Pallas kernels for 0%

profile of v1, /device:TPU:1, one launch (start us, length us, event | category | flops | bytes accessed | tf_op | source)
XLA Modules:
  0.0 565.8 jit_solution(10794712265586953237)
XLA Ops:
  0.0 5.4 copy.13
  5.4 161.4 %all_to_all.20 = bf16[16,850,256]{2,1,0:T(8,128)(2,1)S(1)} all-to-all(bf16[16,850,256]{2,1,0:T(8,128)(2,1)S(1)} %copy.13), channel_id=1, replica_groups=mesh['groups'=2,'aux'=16] {'aux'}, dimensions={0} | all-to-all | bytes 13926400 | tf_op jit(solution)/shard_map/all_to_all | solution.py:23
  166.8 0.0 copy-start
  166.8 1.4 copy.24
  168.3 1.5 copy-done
  169.7 0.5 pad
  170.2 0.0 copy-start.4
  170.2 0.0 copy-start.3
  170.2 0.0 copy-start.2
  170.2 7.5 %copy.19 = bf16[107,8,16,256]{3,1,2,0:T(8,128)(2,1)} copy(bf16[107,8,16,256]{3,2,1,0:T(8,128)(2,1)S(1)} %bitcast.49) | data formatting | bytes 14024704
  177.8 0.0 collective-permute-start
  177.8 0.0 copy-done.4
  177.8 0.7 dynamic_slice.15
  178.4 0.0 copy-done.3
  178.4 0.6 dynamic_slice.16
  179.7 76.5 %collective-permute-done = bf16[850,4096]{1,0:T(8,128)(2,1)} collective-permute-done((bf16[850,4096]{1,0:T(8,128)(2,1)}, bf16[850,4096]{1,0:T(8,128)(2,1)}, u32[]{:S(2)}, u32[]{:S(2)}) %collective-permute-start) | collective-permute-done | bytes 6963232 | tf_op jit(solution)/shard_map/ppermute | solution.py:10
  256.2 0.0 copy-done.2
  256.2 10.8 %conditional.1 = (bf16[850,4096]{1,0:T(8,128)(2,1)}, f32[850,4096]{1,0:T(8,128)}) conditional(s32[]{:T(128)} %bitcast.9, () %tuple.24, (bf16[850,4096]{1,0:T(8,128)(2,1)}, bf16[850,4096]{1,0:T(8,128)(2,1)}, s32[]{:T(128)}, f32[16]{0:T(128)S(1)}, f32[]{:T(128)}, /*index=5*/f32[850]{0:T(1024)S(1)}, s32[]{:T(128)}) %tuple.32), branch_computations={%region_0.1_spmd, %region_1.2_spmd.clone} | conditional | flops 17776721920 | bytes 80553024 | solution.py:46
  256.2 6.8 %broadcast_in_dim.4 = f32[850,4096]{1,0:T(8,128)} broadcast(f32[]{:T(128)} %constant.35.clone), dimensions={} | broadcast | bytes 13926404 | tf_op jit(solution)/shard_map/broadcast_in_dim | solution.py:33
  263.0 3.8 broadcast_in_dim.1
  267.0 34.0 %collective-permute-start.1 = (bf16[850,4096]{1,0:T(8,128)(2,1)}, bf16[850,4096]{1,0:T(8,128)(2,1)}, u32[]{:S(2)}, u32[]{:S(2)}) collective-permute-start(bf16[850,4096]{1,0:T(8,128)(2,1)} %get-tuple-element.126), channel_id=1, source_target_pairs={{15,0},{0,1},{1,2},{2,3},{3,4},{4,5},{5,6},{6,7},{7,8},{8,9},{9,10... | collective-permute-start | bytes 20889608 | tf_op jit(solution)/shard_map/ppermute | solution.py:10
  302.4 10.8 %fusion.5 = f32[850,850,1]{1,0,2:T(8,128)S(1)} fusion(bf16[16,850,256]{2,1,0:T(8,128)(2,1)} %copy-done), kind=kOutput, calls=%fused_computation.8 | convolution fusion | flops 5918720000 | bytes 9853200 | tf_op jit(solution)/shard_map/dot_general | solution.py:14
  313.2 3.0 copy.14
  316.2 15.1 %fusion.9 = f32[850,4096]{1,0:T(8,128)} fusion(bf16[850,4096]{1,0:T(8,128)(2,1)} %bitcast.18, f32[850,850,1]{1,0,2:T(8,128)S(1)} %fusion.5, f32[850,850]{0,1:T(8,128)} %copy.14, f32[850]{0:T(1024)S(1)} %copy-done.2, f32[850]{0:T(1024)S(1)} %broadcast_subtract_fusion.1), kind=kOutput, calls=%fused_computation.15 | convolution fusion | flops 5923777536 | bytes 26676400 | tf_op jit(solution)/shard_map/dot_general | solution.py:32
  331.2 45.7 %collective-permute-done.1 = bf16[850,4096]{1,0:T(8,128)(2,1)} collective-permute-done((bf16[850,4096]{1,0:T(8,128)(2,1)}, bf16[850,4096]{1,0:T(8,128)(2,1)}, u32[]{:S(2)}, u32[]{:S(2)}) %collective-permute-start.1) | collective-permute-done | bytes 6963232 | tf_op jit(solution)/shard_map/ppermute | solution.py:10
  376.9 12.7 %add_convert_fusion = bf16[850,4096]{1,0:T(8,128)(2,1)S(1)} fusion(bf16[850,4096]{1,0:T(8,128)(2,1)} %collective-permute-done.1, f32[850,4096]{1,0:T(8,128)} %fusion.9, f32[850,4096]{1,0:T(8,128)} %get-tuple-element.125), kind=kLoop, calls=%fused_computation.7 | loop fusion | flops 13926400 | bytes 41779200 | tf_op jit(solution)/shard_map/convert_element_type | solution.py:49
  389.6 2.6 copy.20
  392.2 3.4 slice
  395.6 5.4 copy.23
  401.0 160.0 %all_to_all.21 = bf16[16,850,256]{2,1,0:T(8,128)(2,1)S(1)} all-to-all(bf16[16,850,256]{2,1,0:T(8,128)(2,1)S(1)} %bitcast.48), channel_id=1, replica_groups=mesh['groups'=2,'aux'=16] {'aux'}, dimensions={0} | all-to-all | bytes 13926400 | tf_op jit(solution)/shard_map/all_to_all | solution.py:51
  561.0 4.3 copy.17
  (1 shorter events, 0.0 us)
Async XLA Ops:
  166.8 2.9 copy-start
  170.2 7.6 %copy-start.4 = (f32[16]{0:T(128)S(1)}, f32[16]{0:T(128)}, u32[]{:S(2)}) copy-start(f32[16]{0:T(128)} %param.7) | copy-start | bytes 196
  170.2 8.2 %copy-start.3 = (s32[16]{0:T(128)S(1)}, s32[16]{0:T(128)}, u32[]{:S(2)}) copy-start(s32[16]{0:T(128)} %param.9) | copy-start | bytes 196
  170.2 86.0 %copy-start.2 = (f32[850]{0:T(1024)S(1)}, f32[850]{0:T(1024)}, u32[]{:S(2)}) copy-start(f32[850]{0:T(1024)} %param.8) | copy-start | bytes 10204
  177.8 78.4 %collective-permute-start = (bf16[850,4096]{1,0:T(8,128)(2,1)}, bf16[850,4096]{1,0:T(8,128)(2,1)}, u32[]{:S(2)}, u32[]{:S(2)}) collective-permute-start(bf16[850,4096]{1,0:T(8,128)(2,1)} %bitcast.18), channel_id=1, source_target_pairs={{1,0},{2,1},{3,2},{4,3},{5,4},{6,5},{7,6},{8,7},{9,8},{10,9},{11,1... | collective-permute-start | bytes 20889608 | tf_op jit(solution)/shard_map/ppermute | solution.py:10
  267.0 110.0 %collective-permute-start.1 = (bf16[850,4096]{1,0:T(8,128)(2,1)}, bf16[850,4096]{1,0:T(8,128)(2,1)}, u32[]{:S(2)}, u32[]{:S(2)}) collective-permute-start(bf16[850,4096]{1,0:T(8,128)(2,1)} %get-tuple-element.126), channel_id=1, source_target_pairs={{15,0},{0,1},{1,2},{2,3},{3,4},{4,5},{5,6},{6,7},{7,8},{8,9},{9,10... | collective-permute-start | bytes 20889608 | tf_op jit(solution)/shard_map/ppermute | solution.py:10

commit v2 on v0

v2 whole, which is shorter than its diff:
```python
import functools

import jax
import jax.numpy as jnp
from jax import lax
from jax.experimental import pallas as pl
from jax.experimental.pallas import tpu as pltpu
from jax.sharding import PartitionSpec as P

PLANES = 4
STRIP = 256
MESH = pl.DeviceIdType.MESH
F32, BF16 = jnp.float32, jnp.bfloat16


def up_to(size, unit):
    return -(-size // unit) * unit


def kernel(
    m, k, occ_ref, kept_ref, vrow_ref, vcol_ref, x_ref, out_ref,
    bs, cbuf, rbuf, xbuf, tt, gbuf,
    b_send, b_recv, b_local, s12, s3, r13, r2, t_send, t_recv, g_send, g_recv, g_local,
):
    occ, nvp, qd = x_ref.shape
    nvr = out_ref.shape[1]
    me = lax.axis_index("aux")
    plane, q = me // m, me % m
    first = plane * m
    outer = (plane == 0) | (plane == PLANES - 1)
    side = plane // 2
    hop_plane = jnp.where(outer, 1 + side, 3 * side)
    hop = {"aux": hop_plane * m + q}
    across = {"aux": (3 - plane) * m + q}
    strips = [(a, min(a + STRIP, nvp)) for a in range(0, nvp, STRIP)]

    barrier = pltpu.get_barrier_semaphore()
    for d in range(1, m):
        peer = first + (q + d) % m
        pl.semaphore_signal(barrier, inc=1, device_id={"aux": peer}, device_id_type=MESH)
    pl.semaphore_signal(barrier, inc=1, device_id=hop, device_id_type=MESH)

    @pl.when(jnp.logical_not(outer))
    def _():
        pl.semaphore_signal(barrier, inc=1, device_id=across, device_id_type=MESH)
        pl.semaphore_wait(barrier, m + 1)

    @pl.when(outer)
    def _():
        pl.semaphore_wait(barrier, m)

    def lanes(p):
        return pl.ds(pl.multiple_of(p * qd, qd), qd)

    def b_copy(slot, d):
        p = (q + d) % m
        return pltpu.make_async_remote_copy(
            src_ref=x_ref.at[(k * p + slot) % occ], dst_ref=bs.at[slot, :, lanes(q)],
            send_sem=b_send.at[slot, d - 1], recv_sem=b_recv.at[slot, d - 1],
            device_id={"aux": first + p}, device_id_type=MESH,
        )

    def b_own(slot):
        return pltpu.make_async_copy(
            x_ref.at[(k * q + slot) % occ], bs.at[slot, :, lanes(q)], b_local.at[slot]
        )

    def b_wait(slot):
        b_own(slot).wait()
        for d in range(1, m):
            p = (q + m - d) % m
            pltpu.make_async_remote_copy(
                src_ref=x_ref.at[0], dst_ref=bs.at[slot, :, lanes(p)],
                send_sem=b_send.at[slot, d - 1], recv_sem=b_recv.at[slot, d - 1],
                device_id={"aux": first + p}, device_id_type=MESH,
            ).wait_recv()

    @pl.loop(0, k + 1)
    def _(i):
        slot = jnp.where(i < 2, k - 1 + i, i - 2)
        b_own(slot).start()
        for d in range(1, m):
            b_copy(slot, d).start()

    def piece(buf, unit, kind, c):
        a, b = strips[c]
        return buf.at[unit, a:b, (0 if kind else a) : nvp]

    def hop_copy(src, dst, send, recv, target, unit, kind, c):
        return pltpu.make_async_remote_copy(
            src_ref=piece(src, unit, kind, c), dst_ref=piece(dst, unit, kind, c),
            send_sem=send.at[unit, c], recv_sem=recv.at[unit, c],
            device_id=target, device_id_type=MESH,
        )

    def inward(unit, kind, c):
        return hop_copy(cbuf, rbuf, s12, r13, hop, unit, kind, c)

    def exchange(unit, kind, c):
        return hop_copy(cbuf, xbuf, s12, r2, across, unit, kind, c)

    def outward(unit, kind, c):
        return hop_copy(rbuf, rbuf, s3, r13, hop, unit, kind, c)

    def partial(r, kind):
        s = (r + k - 1) % k
        unit = 2 * r + kind
        for c, (a, b) in enumerate(strips):
            low = 0 if kind else a
            got = lax.dot_general(
                bs[s, a:b, :], bs[s + kind, low:nvp, :], (((1,), (1,)), ((), ())),
                preferred_element_type=F32,
            )
            piece(cbuf, unit, kind, c)[...] = got.astype(BF16)

            @pl.when(outer)
            def _():
                inward(unit, kind, c).start()

        @pl.when(jnp.logical_not(outer))
        def _():
            for c in range(len(strips)):
                inward(unit, kind, c).wait_recv()
                mine, theirs = piece(cbuf, unit, kind, c), piece(rbuf, unit, kind, c)
                mine[...] = (mine[...].astype(F32) + theirs[...].astype(F32)).astype(BF16)
                exchange(unit, kind, c).start()

    def energies(r, kind):
        s = (r + k - 1) % k
        i = (k * q + s) % occ
        j = (i + kind) % occ
        return occ_ref[i] + occ_ref[j], kept_ref[i] == 1

    def t_block(unit, e, a, b, c, d):
        coulomb = cbuf[unit, a:b, c:d].astype(F32) + xbuf[unit, a:b, c:d].astype(F32)
        return coulomb / (e - vcol_ref[a:b, :] - vrow_ref[:, c:d])

    def u_diag(r):
        unit = 2 * r
        e, _ = energies(r, 0)
        for c, (a, b) in enumerate(strips):
            exchange(unit, 0, c).wait_recv()
            rbuf[unit, a:b, a:nvp] = t_block(unit, e, a, b, a, nvp).astype(BF16)
            outward(unit, 0, c).start()

    def u_pair(r):
        unit = 2 * r + 1
        e, flag = energies(r, 1)
        for c in range(len(strips)):
            exchange(unit, 1, c).wait_recv()
        for c, (a, b) in enumerate(strips):
            for a2, b2 in strips[c:]:
                upper = t_block(unit, e, a, b, a2, b2)
                lower = upper if a2 == a else t_block(unit, e, a2, b2, a, b)
                u = jnp.where(flag, 2.0 * upper - lower.T, 0.0)
                rbuf[unit, a:b, a2:b2] = u.astype(BF16)
                if a2 != a:
                    u = jnp.where(flag, 2.0 * lower - upper.T, 0.0)
                    rbuf[unit, a2:b2, a:b] = u.astype(BF16)
            outward(unit, 1, c).start()

    def t_copy():
        return pltpu.make_async_remote_copy(
            src_ref=tt.at[0], dst_ref=tt.at[1], send_sem=t_send, recv_sem=t_recv,
            device_id={"aux": first + (q + 1) % m}, device_id_type=MESH,
        )

    def g_copy(s, d):
        p = (q + d) % m
        return pltpu.make_async_remote_copy(
            src_ref=gbuf.at[s, 0:nvr, lanes(p)], dst_ref=out_ref.at[k * q + s, 0:nvr, :],
            send_sem=g_send.at[s, d - 1], recv_sem=g_recv.at[s, d - 1],
            device_id={"aux": first + p}, device_id_type=MESH,
        )

    def g_own(s):
        return pltpu.make_async_copy(
            gbuf.at[s, 0:nvr, lanes(q)], out_ref.at[k * q + s, 0:nvr, :], g_local.at[s]
        )

    def density(r):
        s = (r + k - 1) % k
        diag = 2 * (r % k)

        @pl.when(r < k)
        def _():
            @pl.when(outer)
            def _():
                for kind in (0, 1):
                    for c in range(len(strips)):
                        outward(2 * r + kind, kind, c).wait_recv()

            for c, (a, b) in enumerate(strips):
                for a2, b2 in strips[c + 1 :]:
                    mirrored = rbuf[diag, a:b, a2:b2].astype(F32).T
                    rbuf[diag, a2:b2, a:b] = mirrored.astype(BF16)

        @pl.when(r == 1)
        def _():
            t_copy().wait_recv()

        @pl.when(r >= 1)
        def _():
            for a, b in strips:
                total = jnp.dot(rbuf[diag, a:b, :], bs[s], preferred_element_type=F32)
                total += jnp.dot(rbuf[diag + 1, a:b, :], bs[s + 1], preferred_element_type=F32)
                gbuf[s, a:b, :] = (total + tt[1, a:b, :].astype(F32)).astype(BF16)
            g_own(s).start()
            for d in range(1, m):
                g_copy(s, d).start()

        @pl.when(r < k)
        def _():
            where = jnp.where(r == 0, 0, 1)
            for a, b in strips:
                got = lax.dot_general(
                    rbuf[diag + 1, :, a:b], bs[s], (((0,), (0,)), ((), ())),
                    preferred_element_type=F32,
                )
                tt[where, a:b, :] = got.astype(BF16)

        @pl.when(r == 0)
        def _():
            t_copy().start()

    @pl.loop(0, k + 2)
    def _(r):
        s = (r + k - 1) % k

        @pl.when(r <= 1)
        def _():
            b_wait(s)

        @pl.when(r < k)
        def _():
            partial(r, 0)

        @pl.when((r >= 1) & (r <= k) & jnp.logical_not(outer))
        def _():
            u_pair(r - 1)

        @pl.when(r < k - 1)
        def _():
            b_wait(s + 1)

        @pl.when(r < k)
        def _():
            partial(r, 1)

        @pl.when((r < k) & jnp.logical_not(outer))
        def _():
            u_diag(r)

        @pl.when(r >= 1)
        def _():
            density(r - 1)

    t_copy().wait_send()

    @pl.loop(0, k + 1)
    def _(slot):
        for d in range(1, m):
            b_copy(slot, d).wait_send()

    @pl.loop(0, k)
    def _(s):
        for kind in (0, 1):
            for c in range(len(strips)):
                inward(2 * s + kind, kind, c).wait_send()

        @pl.when(jnp.logical_not(outer))
        def _():
            for kind in (0, 1):
                for c in range(len(strips)):
                    outward(2 * s + kind, kind, c).wait_send()

        g_own(s).wait()
        for d in range(1, m):
            g_copy(s, d).wait_send()
            p = (q + m - d) % m
            pltpu.make_async_remote_copy(
                src_ref=gbuf.at[s, 0:nvr, lanes(p)], dst_ref=out_ref.at[k * p + s, 0:nvr, :],
                send_sem=g_send.at[s, d - 1], recv_sem=g_recv.at[s, d - 1],
                device_id={"aux": first + p}, device_id_type=MESH,
            ).wait_recv()


def body(b_factors, occ_energy, vir_energy, kept):
    occ, nv, qd = b_factors.shape
    m = lax.axis_size("aux") // PLANES
    k = occ // m
    nvp, nvr = up_to(nv, 128), up_to(nv, 16)
    x = jnp.pad(b_factors, ((0, 0), (0, nvp - nv), (0, 0)))
    vir = jnp.pad(vir_energy, (0, nvp - nv), constant_values=1.0)
    pieces = len(range(0, nvp, STRIP))
    square = pltpu.VMEM((2 * k, nvp, nvp), BF16)
    dma = pltpu.SemaphoreType.DMA
    flops = 2 * nvp * nvp * m * qd * 5 * k
    out = pl.pallas_call(
        functools.partial(kernel, m, k),
        out_shape=jax.ShapeDtypeStruct((occ, nvr, qd), BF16),
        in_specs=[pl.BlockSpec(memory_space=pltpu.SMEM)] * 2
        + [pl.BlockSpec(memory_space=pltpu.VMEM)] * 2
        + [pl.BlockSpec(memory_space=pl.ANY)],
        out_specs=pl.BlockSpec(memory_space=pl.ANY),
        scratch_shapes=[
            pltpu.VMEM((k + 1, nvp, m * qd), BF16), square, square, square,
            pltpu.VMEM((2, nvp, m * qd), BF16), pltpu.VMEM((k, nvp, m * qd), BF16),
            dma((k + 1, m - 1)), dma((k + 1, m - 1)), dma((k + 1,)),
            dma((2 * k, pieces)), dma((2 * k, pieces)), dma((2 * k, pieces)), dma((2 * k, pieces)),
            dma, dma, dma((k, m - 1)), dma((k, m - 1)), dma((k,)),
        ],
        compiler_params=pltpu.CompilerParams(
            collective_id=0, has_side_effects=True, vmem_limit_bytes=63 * 2**20
        ),
        cost_estimate=pl.CostEstimate(flops=flops, bytes_accessed=4 * x.size, transcendentals=0),
    )(occ_energy, kept, vir[None, :], vir[:, None], x)
    return out[:, :nv]


def solution(mesh):
    placed = (P("groups", None, "aux"), P("groups"), P("groups"), P("groups"))
    return jax.shard_map(
        body, mesh=mesh, in_specs=placed, out_specs=P("groups", None, "aux"), check_vma=False
    )
```

time: 828 us -> 358 us (0.43); the launches traced: 814 us -> 358 us
  Pallas kernels: 0 us -> 339 us
  blocking collectives: 321 us -> 0 us
  other arithmetic: 178 us -> 0 us
  waiting for transfers between devices: 125 us -> 0 us
  local copies, waits for them, and re-layouts: 132 us -> 18.7 us
  starting transfers between devices: 31.9 us -> 0 us
  matrix products: 22.9 us -> 0 us
    pallas_call x0 -> x1, Pallas kernels: none -> 339 us  [body(): pl.pallas_call(functools.partial(kernel, m, k), out_shape=jax.ShapeDtypeS...]
    all_to_all x2 -> x0, blocking collectives: 321 us -> none  [the longest x1 161 us: body(): lax.all_to_all(b_factors, 'aux', split_axis=0, concat_axis=2, tiled=True)[0]]
    unnamed x1 -> x0, other arithmetic: 158 us -> none
    ppermute x2 -> x0, waiting for transfers between devices: 125 us -> none  [passed_along(): return lax.ppermute(block, axis, route)]
    unnamed x15 -> x1, local copies, waits for them, and re-layouts: 69.1 us -> 5.49 us
    broadcast_in_dim x3 -> x2, local copies, waits for them, and re-layouts: 45.7 us -> 1.54 us  [the longest x1 0.95 us: body(): vir[:, None]]
    ppermute x2 -> x0, starting transfers between devices: 31.9 us -> none  [passed_along(): return lax.ppermute(block, axis, route)]
    dot_general x2 -> x0, matrix products: 22.9 us -> none  [the longest x1 12.2 us: body(): diag = jnp.dot(u_own, owned, preferred_element_type=jnp.float32)]
  transfers between devices with their start and end apart: 2 -> 0, of which waited for: 2 -> 0; matrix products, arithmetic and copies ran while one was open for 3% -> 0% of each run, Pallas kernels for 0% -> 0%
where the time goes in v2:
time: 358 us
  Pallas kernels  339 us (95%)
  local copies, waits for them, and re-layouts  18.7 us (5%)
    pallas_call x1, Pallas kernels, body(): pl.pallas_call(functools.partial(kernel, m, k), out_shape=jax.ShapeDtypeS...  339 us
    slice x3, local copies, waits for them, and re-layouts, body(): return out[:, :nv]  7.3 us

profile of v2, /device:TPU:1, one launch (start us, length us, event | category | flops | bytes accessed | tf_op | source)
XLA Modules:
  0.0 357.9 jit_solution(3507302058594752798)
XLA Ops:
  0.0 0.7 pad.8
  0.7 0.6 broadcast_in_dim.6.vrow_ref
  1.3 1.0 broadcast_in_dim.8.vcol_ref
  2.2 5.5 %copy.7 = bf16[16,850,256]{2,1,0:T(8,128)(2,1)S(1)} copy(bf16[16,850,256]{2,0,1:T(8,128)(2,1)} %param.4) | data formatting | bytes 13926400 | tf_op args[0]
  7.7 3.7 %pad.9.x_ref = bf16[16,896,256]{2,1,0:T(8,128)(2,1)} pad(bf16[16,850,256]{2,1,0:T(8,128)(2,1)S(1)} %copy.7, bf16[]{:T(256)} %constant.4.clone.1), padding=0_0x0_46x0_0 | pad | bytes 14303234 | tf_op jit(solution)/shard_map/jit(_pad)/pad | solution.py:293
  11.4 339.2 %shard_map.46 = bf16[16,864,256]{2,1,0:T(8,128)(2,1)} custom-call(f32[16]{0:T(128)} %occ_ref.1, s32[16]{0:T(128)} %kept_ref.1, f32[1,896]{1,0:T(1,128)} %broadcast_in_dim.6.vrow_ref, f32[896,1]{1,0:T(8,128)} %broadcast_in_dim.8.vcol_ref, bf16[16,896,256]{2,1,0:T(8,128)(2,1)} %pad.9.x_ref), custom_call_target="tpu_custom_call" | custom-call | flops 32883343360 | bytes 14680064 | tf_op jit(solution)/shard_map/pallas_call | solution.py:299
  350.6 0.0 slice-start
  350.6 3.0 slice-done
  353.6 4.3 %copy.9 = bf16[16,850,256]{2,0,1:T(8,128)(2,1)} copy(bf16[16,850,256]{2,1,0:T(8,128)(2,1)S(1)} %slice-done) | data formatting | bytes 13926400 | tf_op jit(solution)/shard_map/slice | solution.py:318
Async XLA Ops:
  350.6 3.0 slice-start

commit v3 on v2

--- a/solution.py
+++ b/solution.py
@@ -8,7 +8,7 @@
 from jax.sharding import PartitionSpec as P
 
 PLANES = 4
-STRIP = 256
+STRIP, WIDE = 128, 256
 MESH = pl.DeviceIdType.MESH
 F32, BF16 = jnp.float32, jnp.bfloat16
 
@@ -32,7 +32,11 @@
     hop_plane = jnp.where(outer, 1 + side, 3 * side)
     hop = {"aux": hop_plane * m + q}
     across = {"aux": (3 - plane) * m + q}
-    strips = [(a, min(a + STRIP, nvp)) for a in range(0, nvp, STRIP)]
+    strips = [(a, a + STRIP) for a in range(0, nvp, STRIP)]
+    wide = [(a, min(a + WIDE, nvp)) for a in range(0, nvp, WIDE)]
+
+    for unit in range(1, 2 * k, 2):
+        xbuf[unit, nvr:nvp, :] = jnp.zeros((nvp - nvr, nvp), BF16)
 
     barrier = pltpu.get_barrier_semaphore()
     for d in range(1, m):
@@ -75,16 +79,16 @@
                 device_id={"aux": first + p}, device_id_type=MESH,
             ).wait_recv()
 
-    @pl.loop(0, k + 1)
-    def _(i):
-        slot = jnp.where(i < 2, k - 1 + i, i - 2)
+    def b_start(slot):
         b_own(slot).start()
         for d in range(1, m):
             b_copy(slot, d).start()
+
+    b_start(k - 1)
 
     def piece(buf, unit, kind, c):
         a, b = strips[c]
-        return buf.at[unit, a:b, (0 if kind else a) : nvp]
+        return buf.at[unit, a : min(b, nvr), (0 if kind else a) : nvp]
 
     def hop_copy(src, dst, send, recv, target, unit, kind, c):
         return pltpu.make_async_remote_copy(
@@ -102,7 +106,7 @@
     def outward(unit, kind, c):
         return hop_copy(rbuf, rbuf, s3, r13, hop, unit, kind, c)
 
-    def partial(r, kind):
+    def partial(r, kind, before, between):
         s = (r + k - 1) % k
         unit = 2 * r + kind
         for c, (a, b) in enumerate(strips):
@@ -111,10 +115,15 @@
                 bs[s, a:b, :], bs[s + kind, low:nvp, :], (((1,), (1,)), ((), ())),
                 preferred_element_type=F32,
             )
-            piece(cbuf, unit, kind, c)[...] = got.astype(BF16)
+            cbuf[unit, a:b, low:nvp] = got.astype(BF16)
 
             @pl.when(outer)
             def _():
+                @pl.when(unit > 0)
+                def _():
+                    earlier = jnp.maximum(2 * r - 2 * before[0], 0) + before[1]
+                    inward(earlier, before[1], c).wait_send()
+
                 inward(unit, kind, c).start()
 
         @pl.when(jnp.logical_not(outer))
@@ -124,6 +133,8 @@
                 mine, theirs = piece(cbuf, unit, kind, c), piece(rbuf, unit, kind, c)
                 mine[...] = (mine[...].astype(F32) + theirs[...].astype(F32)).astype(BF16)
                 exchange(unit, kind, c).start()
+                if c == 0:
+                    between()
 
     def energies(r, kind):
         s = (r + k - 1) % k
@@ -139,6 +150,7 @@
         unit = 2 * r
         e, _ = energies(r, 0)
         for c, (a, b) in enumerate(strips):
+            b = min(b, nvr)
             exchange(unit, 0, c).wait_recv()
             rbuf[unit, a:b, a:nvp] = t_block(unit, e, a, b, a, nvp).astype(BF16)
             outward(unit, 0, c).start()
@@ -178,52 +190,82 @@
             gbuf.at[s, 0:nvr, lanes(q)], out_ref.at[k * q + s, 0:nvr, :], g_local.at[s]
         )
 
+    def diag_ready(r):
+        unit = 2 * r
+
+        @pl.when(outer)
+        def _():
+            for c in range(len(strips)):
+                outward(unit, 0, c).wait_recv()
+
+        for c, (a, b) in enumerate(strips):
+            for a2, b2 in strips[c + 1 :]:
+                mirrored = rbuf[unit, a:b, a2:b2].astype(F32).T
+                rbuf[unit, a2:b2, a:b] = mirrored.astype(BF16)
+
+    def pair_ready(r):
+        @pl.when(outer)
+        def _():
+            for c in range(len(strips)):
+                outward(2 * r + 1, 1, c).wait_recv()
+
+    def gamma(s, diag, given):
+        for a, b in wide:
+            b = min(b, nvr)
+            total = jnp.dot(rbuf[diag, a:b, :], bs[s], preferred_element_type=F32)
+            total += jnp.dot(rbuf[diag + 1, a:b, :], bs[s + 1], preferred_element_type=F32)
+            gbuf[s, a:b, :] = (total + tt[given, a:b, :].astype(F32)).astype(BF16)
+        g_own(s).start()
+        for d in range(1, m):
+            g_copy(s, d).start()
+
+    def to_next(r, where):
+        s = (r + k - 1) % k
+        for a, b in wide:
+            got = lax.dot_general(
+                rbuf[2 * r + 1, 0:nvr, a:b], bs[s, 0:nvr, :], (((0,), (0,)), ((), ())),
+                preferred_element_type=F32,
+            )
+            tt[where, a:b, :] = got.astype(BF16)
+
     def density(r):
-        s = (r + k - 1) % k
-        diag = 2 * (r % k)
-
-        @pl.when(r < k)
-        def _():
-            @pl.when(outer)
-            def _():
-                for kind in (0, 1):
-                    for c in range(len(strips)):
-                        outward(2 * r + kind, kind, c).wait_recv()
-
-            for c, (a, b) in enumerate(strips):
-                for a2, b2 in strips[c + 1 :]:
-                    mirrored = rbuf[diag, a:b, a2:b2].astype(F32).T
-                    rbuf[diag, a2:b2, a:b] = mirrored.astype(BF16)
+        last = r == k - 1
+
+        @pl.when(last)
+        def _():
+            t_copy().wait_send()
+
+        pair_ready(r)
+
+        @pl.when(r < k - 1)
+        def _():
+            diag_ready(r)
 
         @pl.when(r == 1)
         def _():
             t_copy().wait_recv()
 
-        @pl.when(r >= 1)
-        def _():
-            for a, b in strips:
-                total = jnp.dot(rbuf[diag, a:b, :], bs[s], preferred_element_type=F32)
-                total += jnp.dot(rbuf[diag + 1, a:b, :], bs[s + 1], preferred_element_type=F32)
-                gbuf[s, a:b, :] = (total + tt[1, a:b, :].astype(F32)).astype(BF16)
-            g_own(s).start()
-            for d in range(1, m):
-                g_copy(s, d).start()
-
-        @pl.when(r < k)
-        def _():
-            where = jnp.where(r == 0, 0, 1)
-            for a, b in strips:
-                got = lax.dot_general(
-                    rbuf[diag + 1, :, a:b], bs[s], (((0,), (0,)), ((), ())),
-                    preferred_element_type=F32,
-                )
-                tt[where, a:b, :] = got.astype(BF16)
+        @pl.when((r >= 1) & (r < k - 1))
+        def _():
+            gamma(r - 1, 2 * r, 1)
+
+        to_next(r, jnp.where((r == 0) | last, 0, 1))
+
+        @pl.when(last)
+        def _():
+            @pl.loop(0, 2)
+            def _(turn):
+                @pl.when(turn == 1)
+                def _():
+                    diag_ready(r)
+
+                gamma(k - 1 - turn, 2 * r * turn, turn)
 
         @pl.when(r == 0)
         def _():
             t_copy().start()
 
-    @pl.loop(0, k + 2)
+    @pl.loop(0, k + 1)
     def _(r):
         s = (r + k - 1) % k
 
@@ -231,31 +273,43 @@
         def _():
             b_wait(s)
 
-        @pl.when(r < k)
-        def _():
-            partial(r, 0)
-
-        @pl.when((r >= 1) & (r <= k) & jnp.logical_not(outer))
-        def _():
-            u_pair(r - 1)
+            @pl.when(r == 0)
+            def _():
+                b_start(k)
+
+            @pl.when(2 * r < k - 1)
+            def _():
+                b_start(2 * r)
+
+        def pair_before():
+            @pl.when(r >= 1)
+            def _():
+                u_pair(r - 1)
 
         @pl.when(r < k - 1)
         def _():
+            partial(r, 0, (1, 1), pair_before)
             b_wait(s + 1)
-
-        @pl.when(r < k)
-        def _():
-            partial(r, 1)
-
-        @pl.when((r < k) & jnp.logical_not(outer))
-        def _():
-            u_diag(r)
+            later = jnp.where(r == 0, 1, r + 2)
+
+            @pl.when(later < k - 1)
+            def _():
+                b_start(later)
+
+            partial(r, 1, (0, 0), lambda: u_diag(r))
+
+        @pl.when(r == k - 1)
+        def _():
+            partial(r, 1, (1, 1), pair_before)
+            partial(r, 0, (0, 1), lambda: u_pair(r))
+
+            @pl.when(jnp.logical_not(outer))
+            def _():
+                u_diag(r)
 
         @pl.when(r >= 1)
         def _():
             density(r - 1)
-
-    t_copy().wait_send()
 
     @pl.loop(0, k + 1)
     def _(slot):
@@ -264,14 +318,16 @@
 
     @pl.loop(0, k)
     def _(s):
-        for kind in (0, 1):
+        @pl.when(outer & (s == k - 1))
+        def _():
             for c in range(len(strips)):
-                inward(2 * s + kind, kind, c).wait_send()
+                inward(2 * s, 0, c).wait_send()
 
         @pl.when(jnp.logical_not(outer))
         def _():
             for kind in (0, 1):
                 for c in range(len(strips)):
+                    exchange(2 * s + kind, kind, c).wait_send()
                     outward(2 * s + kind, kind, c).wait_send()
 
         g_own(s).wait()

time: 358 us -> 315 us (0.88)
  Pallas kernels: 339 us -> 293 us
    pallas_call x1, Pallas kernels: 339 us -> 293 us  [body(): pl.pallas_call(functools.partial(kernel, m, k), out_shape=jax.ShapeDtypeS...]
where the time goes in v3:
time: 315 us; the launch traced here: 312 us
  Pallas kernels  293 us (93%)
  local copies, waits for them, and re-layouts  18.7 us (6%)
    pallas_call x1, Pallas kernels, body(): pl.pallas_call(functools.partial(kernel, m, k), out_shape=jax.ShapeDtypeS...  293 us
    slice x3, local copies, waits for them, and re-layouts, body(): return out[:, :nv]  7.3 us

profile of v3, /device:TPU:1, one launch (start us, length us, event | category | flops | bytes accessed | tf_op | source)
XLA Modules:
  0.0 312.1 jit_solution(4332396224141330995)
XLA Ops:
  0.0 0.7 pad.8
  0.7 0.6 broadcast_in_dim.6.vrow_ref
  1.3 1.0 broadcast_in_dim.8.vcol_ref
  2.2 5.5 %copy.7 = bf16[16,850,256]{2,1,0:T(8,128)(2,1)S(1)} copy(bf16[16,850,256]{2,0,1:T(8,128)(2,1)} %param.4) | data formatting | bytes 13926400 | tf_op args[0]
  7.7 3.7 %pad.9.x_ref = bf16[16,896,256]{2,1,0:T(8,128)(2,1)} pad(bf16[16,850,256]{2,1,0:T(8,128)(2,1)S(1)} %copy.7, bf16[]{:T(256)} %constant.4.clone.1), padding=0_0x0_46x0_0 | pad | bytes 14303234 | tf_op jit(solution)/shard_map/jit(_pad)/pad | solution.py:349
  11.4 293.4 %shard_map.46 = bf16[16,864,256]{2,1,0:T(8,128)(2,1)} custom-call(f32[16]{0:T(128)} %occ_ref.1, s32[16]{0:T(128)} %kept_ref.1, f32[1,896]{1,0:T(1,128)} %broadcast_in_dim.6.vrow_ref, f32[896,1]{1,0:T(8,128)} %broadcast_in_dim.8.vcol_ref, bf16[16,896,256]{2,1,0:T(8,128)(2,1)} %pad.9.x_ref), custom_call_target="tpu_custom_call" | custom-call | flops 32883343360 | bytes 14680064 | tf_op jit(solution)/shard_map/pallas_call | solution.py:355
  304.8 0.0 slice-start
  304.8 3.0 slice-done
  307.8 4.3 %copy.9 = bf16[16,850,256]{2,0,1:T(8,128)(2,1)} copy(bf16[16,850,256]{2,1,0:T(8,128)(2,1)S(1)} %slice-done) | data formatting | bytes 13926400 | tf_op jit(solution)/shard_map/slice | solution.py:374
Async XLA Ops:
  304.8 3.0 slice-start
